TPU v7x, 32 devices: a whole 2x2x4 slice. The times are simulated.
32 devices in a mesh: groups: 2 (over y), rows: 4 (over z), cols: 2 (over x), sub: 2 (over core).
Axes of the slice: x: 2, y: 2, z: 4, core: 2. Of those that a mesh axis runs over, the one named last changes fastest.
Arguments:
- activations: float32 [2048, 8192], P(('groups', 'rows', 'sub'), 'cols'), parts along dimension 0, may hold values from -72 to 72
- plan: int32 [2, 32], replicated, may hold values from 0 to 31, as said below
Outputs:
- rotated: float32 [2048, 8192], P(('groups', 'rows', 'sub'), 'cols'), parts along dimension 0
There are 2 independent parts, one for each index of `groups`. A program takes and returns all parts, laid end to end along the dimension named above; an argument that names none is the same for every part. Nothing has to cross between parts.
Inputs may be any that keep to these rules, and one draw needn't show every extreme that they name: `plan`: each row is a permutation of the blocks. In row 0 the slots j*16 to (j+1)*16 - 1 hold exactly the blocks numbered j*16 to (j+1)*16 - 1. Row r+1 follows row r by the round-robin move: new slot 0 takes old slot 0, new slot 2 takes old slot 1, new slot 2k (k >= 2) takes old slot 2k-2, new slot 2k+1 takes old slot 2k+3 for k < 15, and new slot 31 takes old slot 30.
All inputs are finite; a program needn't handle non-finite values.
Results may differ from a plain program's by a relative error of at most 0.0014.
Values sent between devices are 32-bit elements; how exact they have to be, the bound alone decides.
No kernel may reach another device: no remote copies, remote signals or barrier semaphores. Data moves between devices by JAX's collectives and lax.ppermute only.
A program may use at most 64 MiB of HBM per device.

v0:
```python
import functools

import jax
import jax.numpy as jnp
from jax import lax
from jax.experimental import pallas as pl
from jax.experimental.pallas import tpu as pltpu
from jax.sharding import PartitionSpec as P

BLK = 256
ROUNDS = 2
PANEL = 64
HALF = 2 * PANEL
SUBLANES = 8

epsilon = 1e-06
HIGH = lax.Precision.HIGHEST
VMEM_LIMIT = 16 * 1024 * 1024
PACK_VMEM_LIMIT = 61 * 1024 * 1024
TEAM_CHIPS = 2
SQUARES = 8
UP_PARTS = 2
CHUNK = 256


def contract(a, b, a_dim, b_dim):
    return lax.dot_general(
        a, b, (((a_dim,), (b_dim,)), ((), ())), precision=HIGH, preferred_element_type=jnp.float32
    )


def iota2(shape, dim):
    return lax.broadcasted_iota(jnp.int32, shape, dim)


def reciprocal(x):
    guess = pl.reciprocal(x, approx=True)
    return guess, 2.0 - x * guess


def eliminate(blocks):
    width = 2 * PANEL
    shape = (SUBLANES, width)
    tiles = PANEL // SUBLANES
    lines = range(SUBLANES)
    ident = jnp.where(
        iota2((PANEL, width), 0) == lax.rem(iota2((PANEL, width), 1), PANEL), 1.0, 0.0
    ).astype(jnp.float32)
    sub = iota2(shape, 0)
    halves = jnp.where(iota2(shape, 1) < PANEL, 0, PANEL)
    whole = jnp.concatenate(blocks, axis=1)
    parts = [whole[SUBLANES * v : SUBLANES * (v + 1)] for v in range(tiles)]
    sides = [ident[SUBLANES * v : SUBLANES * (v + 1)] for v in range(tiles)]
    outs = []

    def spread(tile, line):
        return jnp.broadcast_to(tile[line : line + 1, :], shape)

    for q in range(tiles):
        columns = [
            [
                jnp.take_along_axis(parts[v], halves + (SUBLANES * q + j), axis=1)
                for j in lines
            ]
            for v in range(q, tiles)
        ]
        entry = [[spread(columns[0][j], i) for j in range(i + 1)] for i in lines]
        rows = [spread(parts[q], i) for i in lines]
        side_rows = [spread(sides[q], i) for i in lines]
        inverses = []
        for s in lines:
            guess, mend = reciprocal(entry[s][s])
            inverses.append(guess * mend)
            factors = {i: (entry[i][s] * guess) * mend for i in range(s + 1, SUBLANES)}
            for i in range(s + 1, SUBLANES):
                for j in range(s + 1, i + 1):
                    entry[i][j] = entry[i][j] - factors[i] * entry[j][s]
            for i in range(s + 1, SUBLANES):
                rows[i] = rows[i] - factors[i] * rows[s]
                side_rows[i] = side_rows[i] - factors[i] * side_rows[s]
        for v in range(q + 1, tiles):
            factors = []
            for s in lines:
                value = columns[v - q][s]
                for t in range(s):
                    value = value - factors[t] * entry[s][t]
                factors.append(value * inverses[s])
            for s in lines:
                parts[v] = parts[v] - factors[s] * rows[s]
                sides[v] = sides[v] - factors[s] * side_rows[s]
        tile = side_rows[0] * lax.rsqrt(entry[0][0])
        for i in lines[1:]:
            tile = jnp.where(sub == i, side_rows[i] * lax.rsqrt(entry[i][i]), tile)
        outs.append(tile)
    out = jnp.concatenate(outs, axis=0)
    return out[:, :PANEL], out[:, PANEL:]


def inverse_factors(work_ref):
    lane = iota2((PANEL, BLK), 1)
    line = iota2((PANEL, BLK), 0)
    first_ident = jnp.where(line == lane, 1.0, 0.0).astype(jnp.float32)
    second_ident = jnp.where(line == lane - PANEL, 1.0, 0.0).astype(jnp.float32)
    first_own = lane < PANEL
    own = lane < HALF
    second_own = jnp.logical_and(own, lane >= PANEL)
    lane_below = iota2((HALF, BLK), 1)
    first_own_below = lane_below < PANEL
    own_below = lane_below < HALF

    def step(h, _):
        waiting = jnp.full((PANEL, BLK), h, jnp.int32) == 0
        over = jnp.logical_not(waiting)
        panels = [jnp.concatenate([work_ref[m, h, h], work_ref[m, h, 1 - h]], axis=1) for m in range(2)]
        belows = [
            jnp.concatenate([work_ref[m, 1 - h, h], work_ref[m, 1 - h, 1 - h]], axis=1)
            for m in range(2)
        ]
        invs = eliminate([panel[:PANEL, :PANEL] for panel in panels])
        tops, seconds = [], []
        for m in range(2):
            rows = contract(invs[m], jnp.where(first_own, first_ident, panels[m][:PANEL]), 1, 0)
            factors = jnp.where(jnp.logical_or(own, waiting), rows, 0.0)
            change = contract(factors[:, PANEL:], rows, 0, 0)
            seconds.append(jnp.where(first_own, 0.0, panels[m][PANEL:]) - change[:PANEL])
            belows[m] = jnp.where(first_own_below, 0.0, belows[m]) - change[PANEL:]
            keep = jnp.logical_or(first_own, jnp.logical_and(jnp.logical_not(own), over))
            tops.append(jnp.where(keep, rows, 0.0))
        invs = eliminate([second[:, PANEL:HALF] for second in seconds])
        for m in range(2):
            rows = contract(invs[m], jnp.where(second_own, second_ident, seconds[m]), 1, 0)
            factors = jnp.where(waiting, rows, 0.0)
            change = contract(factors[:, HALF:], rows, 0, 0)
            below = jnp.where(own_below, jnp.where(first_own_below, belows[m], 0.0), belows[m]) - change
            done = jnp.concatenate([tops[m], jnp.where(jnp.logical_or(own, over), rows, 0.0)], axis=0)
            work_ref[m, h, h] = done[:, :HALF]
            work_ref[m, h, 1 - h] = done[:, HALF:]
            work_ref[m, 1 - h, h] = below[:, :HALF]
            work_ref[m, 1 - h, 1 - h] = below[:, HALF:]
        return 0

    lax.fori_loop(0, 2, step, 0)


def pair_terms(blocks_ref, terms_ref):
    tokens = blocks_ref.shape[1]
    chunk = min(CHUNK, tokens)
    line = iota2((SQUARES, BLK), 0)
    terms_ref[...] = jnp.zeros_like(terms_ref)

    def step(i, _):
        at = pl.ds(pl.multiple_of(i * chunk, chunk), chunk)
        upper, lower = blocks_ref[0, at, :], blocks_ref[1, at, :]
        upper_sq = jnp.sum(upper * upper, axis=0, keepdims=True)
        lower_sq = jnp.sum(lower * lower, axis=0, keepdims=True)
        squares = jnp.where(line == 0, upper_sq, jnp.where(line == 1, lower_sq, 0.0))
        terms_ref[:BLK] += contract(upper, lower, 0, 0)
        terms_ref[BLK:] += squares
        return 0

    lax.fori_loop(0, tokens // chunk, step, 0)


SMEM_SPEC = pl.BlockSpec(memory_space=pltpu.SMEM)
VMEM_SPEC = pl.BlockSpec(memory_space=pltpu.VMEM)
HBM_SPEC = pl.BlockSpec(memory_space=pltpu.HBM)


def call(kernel, name, out_shape, in_specs, out_specs, scratch, micros, vmem=VMEM_LIMIT):
    return pl.pallas_call(
        kernel,
        out_shape=out_shape,
        in_specs=in_specs,
        out_specs=out_specs,
        scratch_shapes=scratch,
        compiler_params=pltpu.CompilerParams(vmem_limit_bytes=vmem),
        cost_estimate=pl.CostEstimate(
            flops=int(micros * 1e9), bytes_accessed=1 << 20, transcendentals=0
        ),
        name=name,
    )


def f32(*shape):
    return jax.ShapeDtypeStruct(shape, jnp.float32)


class Layout:
    def __init__(self, block_count):
        self.block_count = block_count
        self.pairs = block_count // 2
        self.subs = lax.axis_size("sub")
        self.columns = lax.axis_size("cols")
        self.token_group = lax.axis_size("rows") * self.subs
        self.team = min(self.pairs, TEAM_CHIPS * self.subs, self.token_group)
        self.teams = self.token_group // self.team
        self.held = self.pairs // self.team
        assert self.team * self.teams == self.token_group
        assert self.team * self.held == self.pairs and self.team & (self.team - 1) == 0
        self.shifts = [0] + list(range(self.team - 1, 0, -1))

    def member(self):
        return lax.rem(lax.axis_index("rows") * self.subs + lax.axis_index("sub"), self.team)

    def partner(self, i):
        return lax.bitwise_xor(self.member(), jnp.int32(self.shifts[i]))

    def place_of(self, member):
        backwards = lax.rem(lax.axis_index("cols"), 2) == 1
        return jnp.where(backwards, self.team - 1 - member, member)

    def pair_at(self, g, i):
        return self.place_of(self.partner(i)) * self.held + g

    def first(self):
        return jnp.logical_and(lax.axis_index("cols") == 0, self.place_of(self.member()) == 0)

    def final(self):
        return jnp.logical_and(
            lax.axis_index("cols") == self.columns - 1,
            self.place_of(self.member()) == self.team - 1,
        )


def pack_kernel(layout, items, plan_ref, x_ref, *refs):
    outs, in_sem = refs[:-1], refs[-1]
    base = lax.axis_index("cols") * layout.block_count
    loads = []
    for i, (item, out) in enumerate(zip(items, outs)):
        pair = layout.pair_at(*item)
        for half in range(2):
            block = plan_ref[0, base + 2 * pair + half] - base
            start = pl.multiple_of(block * BLK, BLK)
            loads.append(
                pltpu.make_async_copy(
                    x_ref.at[:, pl.ds(start, BLK)],
                    out.at[:, half * BLK : (half + 1) * BLK],
                    in_sem.at[2 * i + half],
                )
            )
    for load in loads:
        load.start()
    for load in loads:
        load.wait()


def pack(layout, items, plan, x, vmem):
    count = len(items)
    return call(
        functools.partial(pack_kernel, layout, items),
        "pack",
        [f32(x.shape[0], 2 * BLK)] * count,
        [SMEM_SPEC, HBM_SPEC],
        [VMEM_SPEC] * count,
        [pltpu.SemaphoreType.DMA((2 * count,))],
        2,
        vmem,
    )(plan, x)


def unpack_kernel(layout, *refs):
    pieces, out_ref, held, in_sem, out_sem = refs[:-4], *refs[-4:]
    width = 2 * BLK
    loads, stores = [], []
    for i, piece in enumerate(pieces):
        start = pl.multiple_of(layout.pair_at(*divmod(i, layout.team)) * width, width)
        loads.append(pltpu.make_async_copy(piece, held.at[i], in_sem.at[i]))
        stores.append(
            pltpu.make_async_copy(held.at[i], out_ref.at[:, pl.ds(start, width)], out_sem.at[i])
        )
    for load in loads:
        load.start()
    for load, store in zip(loads, stores):
        load.wait()
        store.start()
    for store in stores:
        store.wait()


def unpack(layout, pieces):
    rows, width = pieces[0].shape
    count = len(pieces)
    return call(
        functools.partial(unpack_kernel, layout),
        "unpack",
        f32(rows, count * width),
        [HBM_SPEC] * count,
        HBM_SPEC,
        [
            pltpu.VMEM((count, rows, width), jnp.float32),
            pltpu.SemaphoreType.DMA((count,)),
            pltpu.SemaphoreType.DMA((count,)),
        ],
        3,
    )(*pieces)


def gather_terms_kernel(layout, *refs):
    pieces, (blocks_ref, terms_ref) = refs[:-2], refs[-2:]
    rows = pieces[0].shape[0]
    for i, piece in enumerate(pieces):
        at = pl.ds(pl.multiple_of(layout.partner(i) * rows, rows), rows)
        blocks_ref[0, at, :] = piece[:, :BLK]
        blocks_ref[1, at, :] = piece[:, BLK:]
    pair_terms(blocks_ref, terms_ref)


def gather_terms(layout, pieces):
    tokens = pieces[0].shape[0] * len(pieces)
    return call(
        functools.partial(gather_terms_kernel, layout),
        "gather_terms",
        [f32(2, tokens, BLK), f32(BLK + SQUARES, BLK)],
        [VMEM_SPEC] * len(pieces),
        [VMEM_SPEC] * 2,
        [],
        2,
    )(*pieces)


def choose_terms_kernel(pick_upper, pick_lower, uppers, lowers, *refs):
    inputs, (blocks_ref, terms_ref) = refs[:-2], refs[-2:]

    def fetch(m, at):
        refs = [inputs[i] for i in at]
        if len(refs[0].shape) == 3:
            pair_ref, inv_ref = refs
            chunk = min(CHUNK, pair_ref.shape[1])

            def step(i, _):
                rows = pl.ds(pl.multiple_of(i * chunk, chunk), chunk)
                blocks_ref[m, rows, :] = turned(pair_ref[0, rows, :], pair_ref[1, rows, :], inv_ref, 0)
                return 0

            lax.fori_loop(0, pair_ref.shape[1] // chunk, step, 0)
        else:
            rows = refs[0].shape[0]
            for i, ref in enumerate(refs):
                blocks_ref[m, i * rows : (i + 1) * rows, :] = ref[...]

    for m, (pick, choices) in enumerate(((pick_upper, uppers), (pick_lower, lowers))):
        chosen = pick()
        pl.when(chosen)(functools.partial(fetch, m, choices[0]))
        pl.when(jnp.logical_not(chosen))(functools.partial(fetch, m, choices[1]))
    pair_terms(blocks_ref, terms_ref)


def choose_terms(picks, uppers, lowers):
    tokens = sum(part.shape[0] for part in uppers[0])
    inputs, places = [], []
    for choice in (*uppers, *lowers):
        places.append(tuple(range(len(inputs), len(inputs) + len(choice))))
        inputs.extend(choice)
    return call(
        functools.partial(choose_terms_kernel, *picks, places[:2], places[2:]),
        "choose_terms",
        [f32(2, tokens, BLK), f32(BLK + SQUARES, BLK)],
        [VMEM_SPEC] * len(inputs),
        [VMEM_SPEC] * 2,
        [],
        2,
    )(*inputs)


def total_terms(refs):
    total = refs[0][...]
    for ref in refs[1:]:
        total = total + ref[...]
    return total


def factor_kernel(*refs):
    terms, (inv_ref, corr_ref, work_ref) = refs[:-3], refs[-3:]
    terms = total_terms(terms)
    square = (BLK, BLK)
    diagonal = iota2(square, 0) == iota2(square, 1)
    upper_sq, lower_sq = terms[BLK : BLK + 1], terms[BLK + 1 : BLK + 2]
    upper_sq = jnp.sum(
        jnp.where(diagonal, jnp.broadcast_to(upper_sq, square), 0.0), axis=1, keepdims=True
    )
    corr = terms[:BLK] * lax.rsqrt(upper_sq + epsilon) * lax.rsqrt(lower_sq + epsilon)
    corr_ref[0] = corr
    corr_ref[1] = -jnp.transpose(corr)

    def gram(m, _):
        corr = corr_ref[m]
        whole = jnp.where(diagonal, 1.0, 0.0).astype(jnp.float32) + contract(corr, corr, 1, 1)
        for r in range(2):
            for c in range(2):
                work_ref[m, r, c] = whole[HALF * r : HALF * (r + 1), HALF * c : HALF * (c + 1)]
        return 0

    def widen(m, _):
        whole = jnp.concatenate(
            [jnp.concatenate([work_ref[m, r, 0], work_ref[m, r, 1]], axis=1) for r in range(2)],
            axis=0,
        )
        inv_ref[m, :, :BLK] = whole
        inv_ref[m, :, BLK:] = contract(whole, corr_ref[m], 1, 0)
        return 0

    lax.fori_loop(0, 2, gram, 0)
    inverse_factors(work_ref)
    lax.fori_loop(0, 2, widen, 0)


def factor(terms):
    return call(
        factor_kernel,
        "factor",
        f32(2, BLK, 2 * BLK),
        [VMEM_SPEC] * len(terms),
        VMEM_SPEC,
        [
            pltpu.VMEM((2, BLK, BLK), jnp.float32),
            pltpu.VMEM((2, 2, 2, HALF, HALF), jnp.float32),
        ],
        11,
    )(*terms)


def turned(own, other, inv_ref, m):
    return contract(own, inv_ref[m, :, :BLK], 1, 1) + contract(other, inv_ref[m, :, BLK:], 1, 1)


def turn_kernel(m, blocks_ref, inv_ref, *out_refs):
    chunk = min(CHUNK, out_refs[0].shape[0])
    for part, out_ref in enumerate(out_refs):
        first = part * out_ref.shape[0]

        def step(i, _):
            start = pl.multiple_of(i * chunk, chunk)
            at = pl.ds(first + start, chunk)
            out_ref[pl.ds(start, chunk), :] = turned(
                blocks_ref[m, at, :], blocks_ref[1 - m, at, :], inv_ref, m
            )
            return 0

        lax.fori_loop(0, out_ref.shape[0] // chunk, step, 0)


def turn(m, blocks, factors, parts=1):
    out = call(
        functools.partial(turn_kernel, m),
        "turn",
        [f32(blocks.shape[1] // parts, BLK)] * parts,
        [VMEM_SPEC] * 2,
        [VMEM_SPEC] * parts,
        [],
        2,
    )(blocks, factors)
    return list(out)


def turn_out_kernel(layout, partners, blocks_ref, inv_ref, *refs):
    outs, out_ref = refs[:-1], refs[-1]
    rows = outs[0].shape[0]
    spans = [pl.ds(pl.multiple_of(layout.partner(i) * rows, rows), rows) for i in partners]

    def step(m, _):
        own = jnp.concatenate([blocks_ref[m, at, :] for at in spans], axis=0)
        other = jnp.concatenate([blocks_ref[1 - m, at, :] for at in spans], axis=0)
        out_ref[m] = turned(own, other, inv_ref, m)
        return 0

    lax.fori_loop(0, 2, step, 0)
    for i, out in enumerate(outs):
        out[:, :BLK] = out_ref[0, i * rows : (i + 1) * rows, :]
        out[:, BLK:] = out_ref[1, i * rows : (i + 1) * rows, :]


def turn_out(layout, partners, blocks, factors):
    rows = blocks.shape[1] // layout.team
    count = len(partners)
    return call(
        functools.partial(turn_out_kernel, layout, partners),
        "turn_out",
        [f32(rows, 2 * BLK)] * count,
        [VMEM_SPEC] * 2,
        [VMEM_SPEC] * count,
        [pltpu.VMEM((2, rows * count, BLK), jnp.float32)],
        2,
    )(blocks, factors)


def on_device(activations, plan):
    token_axes = ("rows", "sub")
    all_axes = ("rows", "cols", "sub")
    layout = Layout(activations.shape[1] // BLK)
    team, teams, held = layout.team, layout.teams, layout.held
    subs, columns, token_group = layout.subs, layout.columns, layout.token_group

    def exchange(pieces):
        arrived = [pieces[0]]
        for shift, piece in zip(layout.shifts[1:], pieces[1:]):
            route = [(t, t ^ shift) for t in range(token_group)]
            arrived.append(lax.ppermute(piece, token_axes, route))
        return arrived

    def shared(terms):
        gathered = [terms]
        for step in range(1, teams):
            route = [(t, (t + step * team) % token_group) for t in range(token_group)]
            gathered.append(lax.ppermute(terms, token_axes, route))
        return gathered

    def along(block, distance):
        route = []
        for at in range(columns * team):
            if 0 <= at + distance < columns * team:
                for group in range(teams):
                    ends = []
                    for one in (at, at + distance):
                        home, inner = divmod(one, team)
                        inner = team - 1 - inner if home % 2 else inner
                        row, sub = divmod(group * team + inner, subs)
                        ends.append((row * columns + home) * subs + sub)
                    route.append(tuple(ends))
        return lax.ppermute(block, all_axes, route)

    def always():
        return lax.axis_index("cols") >= 0

    early = [(0, i) for i in range(1, team)]
    late = [(0, 0)] + [(g, i) for g in range(1, held) for i in range(team)]
    packed = list(pack(layout, early, plan, activations, PACK_VMEM_LIMIT))
    plan, packed[0] = lax.optimization_barrier((plan, packed[0]))
    pieces = dict(zip(early, packed))
    pieces.update(zip(late, pack(layout, late, plan, activations, VMEM_LIMIT)))
    arrived = []
    for g in range(held):
        piece = [pieces[g, i] for i in range(team)]
        if arrived:
            piece, arrived[-1] = lax.optimization_barrier((piece, arrived[-1]))
        arrived.append(exchange(piece))
    ready = [gather_terms(layout, piece) for piece in arrived]
    summed = [shared(terms) for _, terms in ready]
    top = held - 1

    def next_terms(g, uppers, lowers, edge, leaving, arriving):
        if g == 0:
            from_above, pick_upper = (uppers[0], arriving), layout.first
        elif g == 1:
            from_above, pick_upper = (lowers[0], uppers[0]), layout.first
        else:
            from_above, pick_upper = (uppers[g - 1],) * 2, always
        if g == top:
            from_below, pick_lower = (edge, leaving), layout.final
        else:
            from_below, pick_lower = (lowers[g + 1],) * 2, always
        blocks, terms = choose_terms((pick_upper, pick_lower), from_above, from_below)
        return blocks, shared(terms)

    for g in range(1, held):
        summed[0][0], summed[g][0] = lax.optimization_barrier((summed[0][0], summed[g][0]))
    uppers, lowers, nexts = [None] * held, [None] * held, [None] * held
    leaving = None
    for g in range(top):
        factors = factor(summed[g])
        lowers[g] = turn(1, ready[g][0], factors)
        if g == 0:
            leaving = [along(part, -1) for part in lowers[0]]
        uppers[g] = turn(0, ready[g][0], factors)
    factors = factor(summed[top])
    if top:
        nexts[top] = next_terms(top, uppers, lowers, [ready[top][0], factors], leaving, None)
        factors, nexts[top][1][0] = lax.optimization_barrier((factors, nexts[top][1][0]))
    uppers[top] = turn(0, ready[top][0], factors, UP_PARTS)
    if top:
        arriving = [along(part, 1) for part in uppers[top]]
        lowers[top] = turn(1, ready[top][0], factors)
        for term in nexts[top][1]:
            lowers[top][0], term = lax.optimization_barrier((lowers[top][0], term))
    else:
        lowers[0] = turn(1, ready[0][0], factors, UP_PARTS)
        arriving = [
            along(jnp.where(layout.first(), low, up), 1) for low, up in zip(lowers[0], uppers[0])
        ]
        leaving = [along(part, -1) for part in lowers[0]]
    for g in reversed(range(held)):
        if nexts[g] is None:
            nexts[g] = next_terms(g, uppers, lowers, uppers[top], leaving, arriving)

    for g in range(1, held):
        nexts[0][1][0], nexts[g][1][0] = lax.optimization_barrier((nexts[0][1][0], nexts[g][1][0]))
    far = [i for i, shift in enumerate(layout.shifts) if shift >= subs]
    near = [i for i, shift in enumerate(layout.shifts) if shift < subs]
    results = [None] * held
    for g in reversed(range(held)):
        blocks, terms = nexts[g]
        factors = factor(terms)
        sent = [None] * team
        for partners in (far, near):
            if partners:
                for i, piece in zip(partners, turn_out(layout, partners, blocks, factors)):
                    sent[i] = piece
        results[g] = exchange(sent)
    return unpack(layout, [piece for result in results for piece in result])


def solution(mesh):
    in_specs = (P(("groups", "rows", "sub"), "cols"), P())
    out_specs = P(("groups", "rows", "sub"), "cols")
    return jax.shard_map(
        on_device, mesh=mesh, in_specs=in_specs, out_specs=out_specs, check_vma=False
    )
```

profile of v0, /device:TPU:0, one launch (start us, length us, event | category | flops | bytes accessed | tf_op | source)
XLA Modules:
  0.0 141.7 jit_solution(16916046903915794740)
XLA Ops:
  0.0 3.0 %pack.2 = (f32[128,512]{1,0:T(8,128)}, f32[128,512]{1,0:T(8,128)}, f32[128,512]{1,0:T(8,128)}) custom-call(s32[2,32]{1,0:T(2,128)} %plan_ref.2, f32[128,4096]{1,0:T(8,128)} %x_ref.3), custom_call_target="tpu_custom_call" | custom-call | flops 2000000000 | bytes 1048576 | tf_op jit(solution)/shard_map/pack/pallas_call | solution.py:249
  3.0 2.5 %collective-permute-start = (f32[128,512]{1,0:T(8,128)}, f32[128,512]{1,0:T(8,128)S(1)}, u32[]{:S(2)}, u32[]{:S(2)}) collective-permute-start(f32[128,512]{1,0:T(8,128)} %get-tuple-element.56), channel_id=1, source_target_pairs={{0,5},{1,4},{4,1},{5,0},{8,13},{9,12},{12,9},{13,8},{2,7},{3,6},{6... | collective-permute-start | bytes 786440 | tf_op jit(solution)/shard_map/ppermute | solution.py:497
  7.1 5.4 %collective-permute-done.refs_1_ = f32[128,512]{1,0:T(8,128)S(1)} collective-permute-done((f32[128,512]{1,0:T(8,128)}, f32[128,512]{1,0:T(8,128)S(1)}, u32[]{:S(2)}, u32[]{:S(2)}) %collective-permute-start) | collective-permute-done | bytes 262176 | tf_op jit(solution)/shard_map/ppermute | solution.py:497
  12.5 5.7 %collective-permute-done.1.refs_2_ = f32[128,512]{1,0:T(8,128)S(1)} collective-permute-done((f32[128,512]{1,0:T(8,128)}, f32[128,512]{1,0:T(8,128)S(1)}, u32[]{:S(2)}, u32[]{:S(2)}) %collective-permute-start.1) | collective-permute-done | bytes 262176 | tf_op jit(solution)/shard_map/ppermute | solution.py:497
  18.2 2.0 %collective-permute-start.3 = (f32[128,512]{1,0:T(8,128)S(1)}, f32[128,512]{1,0:T(8,128)S(1)}, u32[]{:S(2)}, u32[]{:S(2)}) collective-permute-start(f32[128,512]{1,0:T(8,128)S(1)} %get-tuple-element.66), channel_id=1, source_target_pairs={{0,5},{1,4},{4,1},{5,0},{8,13},{9,12},{12,9},{13,8},{2,7},{3,6},{6... | collective-permute-start | bytes 786440 | tf_op jit(solution)/shard_map/ppermute | solution.py:497
  21.6 2.8 %collective-permute-start.6 = (f32[264,256]{1,0:T(8,128)S(1)}, f32[264,256]{1,0:T(8,128)S(1)}, u32[]{:S(2)}, u32[]{:S(2)}) collective-permute-start(f32[264,256]{1,0:T(8,128)S(1)} %get-tuple-element.70.refs_0_), channel_id=1, source_target_pairs={{0,8},{1,9},{4,12},{5,13},{8,0},{9,1},{12,4},{13,5},{2,10},{3,11},... | collective-permute-start | bytes 811016 | tf_op jit(solution)/shard_map/ppermute | solution.py:504
  24.4 8.0 %collective-permute-done.3.refs_1_ = f32[128,512]{1,0:T(8,128)S(1)} collective-permute-done((f32[128,512]{1,0:T(8,128)S(1)}, f32[128,512]{1,0:T(8,128)S(1)}, u32[]{:S(2)}, u32[]{:S(2)}) %collective-permute-start.3) | collective-permute-done | bytes 262176 | tf_op jit(solution)/shard_map/ppermute | solution.py:497
  32.4 6.1 %collective-permute-done.4.refs_2_ = f32[128,512]{1,0:T(8,128)S(1)} collective-permute-done((f32[128,512]{1,0:T(8,128)S(1)}, f32[128,512]{1,0:T(8,128)S(1)}, u32[]{:S(2)}, u32[]{:S(2)}) %collective-permute-start.4) | collective-permute-done | bytes 262176 | tf_op jit(solution)/shard_map/ppermute | solution.py:497
  39.5 2.2 %collective-permute-start.7 = (f32[264,256]{1,0:T(8,128)S(1)}, f32[264,256]{1,0:T(8,128)S(1)}, u32[]{:S(2)}, u32[]{:S(2)}) collective-permute-start(f32[264,256]{1,0:T(8,128)S(1)} %get-tuple-element.72.refs_0_), channel_id=1, source_target_pairs={{0,8},{1,9},{4,12},{5,13},{8,0},{9,1},{12,4},{13,5},{2,10},{3,11},... | collective-permute-start | bytes 811016 | tf_op jit(solution)/shard_map/ppermute | solution.py:504
  41.7 12.4 %factor.4.inv_ref = f32[2,256,512]{2,1,0:T(8,128)S(1)} custom-call(f32[264,256]{1,0:T(8,128)S(1)} %get-tuple-element.70.refs_0_, f32[264,256]{1,0:T(8,128)S(1)} %collective-permute-done.6.refs_1_), custom_call_target="tpu_custom_call" | custom-call | flops 11000000512 | bytes 1048576 | tf_op jit(solution)/shard_map/factor/pallas_call | solution.py:408
  55.5 1.5 %collective-permute-start.8 = (f32[512,256]{1,0:T(8,128)S(1)}, f32[512,256]{1,0:T(8,128)S(1)}, u32[]{:S(2)}, u32[]{:S(2)}) collective-permute-start(f32[512,256]{1,0:T(8,128)S(1)} %turn.5.refs_0_), channel_id=1, source_target_pairs={{1,0},{9,8},{4,1},{12,9},{5,4},{13,12},{7,5},{15,13},{6,7},{14,15}... | collective-permute-start | bytes 1572872 | tf_op jit(solution)/shard_map/ppermute | solution.py:519
  58.3 12.5 %factor.5.refs_3_.inv_ref = f32[2,256,512]{2,1,0:T(8,128)S(1)} custom-call(f32[264,256]{1,0:T(8,128)S(1)} %get-tuple-element.72.refs_0_, f32[264,256]{1,0:T(8,128)S(1)} %collective-permute-done.7.refs_1_), custom_call_target="tpu_custom_call" | custom-call | flops 11000000512 | bytes 1048576 | tf_op jit(solution)/shard_map/factor/pallas_call | solution.py:408
  73.6 2.8 %collective-permute-start.9 = (f32[256,256]{1,0:T(8,128)S(1)}, f32[256,256]{1,0:T(8,128)S(1)}, u32[]{:S(2)}, u32[]{:S(2)}) collective-permute-start(f32[256,256]{1,0:T(8,128)S(1)} %get-tuple-element.75), channel_id=1, source_target_pairs={{0,1},{8,9},{1,4},{9,12},{4,5},{12,13},{5,7},{13,15},{7,6},{15,14}... | collective-permute-start | bytes 786440 | tf_op jit(solution)/shard_map/ppermute | solution.py:519
  76.4 3.5 %collective-permute-start.10 = (f32[256,256]{1,0:T(8,128)S(1)}, f32[256,256]{1,0:T(8,128)S(1)}, u32[]{:S(2)}, u32[]{:S(2)}) collective-permute-start(f32[256,256]{1,0:T(8,128)S(1)} %get-tuple-element.76), channel_id=1, source_target_pairs={{0,1},{8,9},{1,4},{9,12},{4,5},{12,13},{5,7},{13,15},{7,6},{15,14}... | collective-permute-start | bytes 786440 | tf_op jit(solution)/shard_map/ppermute | solution.py:519
  81.3 6.3 %collective-permute-done.11.refs_1_ = f32[264,256]{1,0:T(8,128)S(1)} collective-permute-done((f32[264,256]{1,0:T(8,128)S(1)}, f32[264,256]{1,0:T(8,128)S(1)}, u32[]{:S(2)}, u32[]{:S(2)}) %collective-permute-start.11) | collective-permute-done | bytes 270368 | tf_op jit(solution)/shard_map/ppermute | solution.py:504
  88.9 12.4 %factor.7.inv_ref = f32[2,256,512]{2,1,0:T(8,128)S(1)} custom-call(f32[264,256]{1,0:T(8,128)S(1)} %get-tuple-element.88.refs_0_, f32[264,256]{1,0:T(8,128)S(1)} %collective-permute-done.11.refs_1_), custom_call_target="tpu_custom_call" | custom-call | flops 11000000512 | bytes 1048576 | tf_op jit(solution)/shard_map/factor/pallas_call | solution.py:408
  102.7 2.0 %collective-permute-start.16 = (f32[128,512]{1,0:T(8,128)S(1)}, f32[128,512]{1,0:T(8,128)S(1)}, u32[]{:S(2)}, u32[]{:S(2)}) collective-permute-start(f32[128,512]{1,0:T(8,128)S(1)} %get-tuple-element.90), channel_id=1, source_target_pairs={{0,5},{1,4},{4,1},{5,0},{8,13},{9,12},{12,9},{13,8},{2,7},{3,6},{6... | collective-permute-start | bytes 786440 | tf_op jit(solution)/shard_map/ppermute | solution.py:497
  104.7 5.6 %collective-permute-start.17 = (f32[128,512]{1,0:T(8,128)S(1)}, f32[128,512]{1,0:T(8,128)S(1)}, u32[]{:S(2)}, u32[]{:S(2)}) collective-permute-start(f32[128,512]{1,0:T(8,128)S(1)} %get-tuple-element.91), channel_id=1, source_target_pairs={{0,4},{1,5},{4,0},{5,1},{8,12},{9,13},{12,8},{13,9},{2,6},{3,7},{6... | collective-permute-start | bytes 786440 | tf_op jit(solution)/shard_map/ppermute | solution.py:497
  111.8 12.4 %factor.6.inv_ref = f32[2,256,512]{2,1,0:T(8,128)S(1)} custom-call(f32[264,256]{1,0:T(8,128)S(1)} %get-tuple-element.82.refs_0_, f32[264,256]{1,0:T(8,128)S(1)} %collective-permute-done.12.refs_1_), custom_call_target="tpu_custom_call" | custom-call | flops 11000000512 | bytes 1048576 | tf_op jit(solution)/shard_map/factor/pallas_call | solution.py:408
  124.2 1.4 turn_out.5
  125.6 1.4 %collective-permute-start.13 = (f32[128,512]{1,0:T(8,128)S(1)}, f32[128,512]{1,0:T(8,128)S(1)}, u32[]{:S(2)}, u32[]{:S(2)}) collective-permute-start(f32[128,512]{1,0:T(8,128)S(1)} %get-tuple-element.84), channel_id=1, source_target_pairs={{0,5},{1,4},{4,1},{5,0},{8,13},{9,12},{12,9},{13,8},{2,7},{3,6},{6... | collective-permute-start | bytes 786440 | tf_op jit(solution)/shard_map/ppermute | solution.py:497
  129.3 4.5 %collective-permute-done.13.refs_1_ = f32[128,512]{1,0:T(8,128)S(1)} collective-permute-done((f32[128,512]{1,0:T(8,128)S(1)}, f32[128,512]{1,0:T(8,128)S(1)}, u32[]{:S(2)}, u32[]{:S(2)}) %collective-permute-start.13) | collective-permute-done | bytes 262176 | tf_op jit(solution)/shard_map/ppermute | solution.py:497
  133.8 6.2 %collective-permute-done.14.refs_2_ = f32[128,512]{1,0:T(8,128)S(1)} collective-permute-done((f32[128,512]{1,0:T(8,128)S(1)}, f32[128,512]{1,0:T(8,128)S(1)}, u32[]{:S(2)}, u32[]{:S(2)}) %collective-permute-start.14) | collective-permute-done | bytes 262176 | tf_op jit(solution)/shard_map/ppermute | solution.py:497
  139.9 1.6 %unpack.1 = f32[128,4096]{1,0:T(8,128)} custom-call(f32[128,512]{1,0:T(8,128)S(1)} %get-tuple-element.83.refs_0_, f32[128,512]{1,0:T(8,128)S(1)} %collective-permute-done.13.refs_1_, f32[128,512]{1,0:T(8,128)S(1)} %collective-permute-done.14.refs_2_, f32[128,512]{1,0:T(8,128)S(1)} %collective-permute-done.15.refs_3_, ...), custom_call_target="tpu_custom_call" | custom-call | flops 3000000000 | bytes 1048576 | tf_op jit(solution)/shard_map/unpack/pallas_call | solution.py:283
  (37 shorter events, 17.0 us)
Async XLA Ops:
  0.0 6.2 %copy-start.1 = (s32[2,32]{1,0:T(2,128)S(1)}, s32[2,32]{1,0:T(2,128)}, u32[]{:S(2)}) copy-start(s32[2,32]{1,0:T(2,128)} %plan_ref.2) | copy-start | bytes 772
  0.0 6.2 %copy-start = (f32[128,4096]{1,0:T(8,128)S(1)}, f32[128,4096]{1,0:T(8,128)}, u32[]{:S(2)}) copy-start(f32[128,4096]{1,0:T(8,128)} %x_ref.3) | copy-start | bytes 6291460
  3.0 9.5 %collective-permute-start = (f32[128,512]{1,0:T(8,128)}, f32[128,512]{1,0:T(8,128)S(1)}, u32[]{:S(2)}, u32[]{:S(2)}) collective-permute-start(f32[128,512]{1,0:T(8,128)} %get-tuple-element.56), channel_id=1, source_target_pairs={{0,5},{1,4},{4,1},{5,0},{8,13},{9,12},{12,9},{13,8},{2,7},{3,6},{6... | collective-permute-start | bytes 786440 | tf_op jit(solution)/shard_map/ppermute | solution.py:497
  5.5 12.7 %collective-permute-start.1 = (f32[128,512]{1,0:T(8,128)}, f32[128,512]{1,0:T(8,128)S(1)}, u32[]{:S(2)}, u32[]{:S(2)}) collective-permute-start(f32[128,512]{1,0:T(8,128)} %get-tuple-element.57), channel_id=1, source_target_pairs={{0,4},{1,5},{4,0},{5,1},{8,12},{9,13},{12,8},{13,9},{2,6},{3,7},{6... | collective-permute-start | bytes 786440 | tf_op jit(solution)/shard_map/ppermute | solution.py:497
  6.2 12.1 %collective-permute-start.2 = (f32[128,512]{1,0:T(8,128)}, f32[128,512]{1,0:T(8,128)S(1)}, u32[]{:S(2)}, u32[]{:S(2)}) collective-permute-start(f32[128,512]{1,0:T(8,128)} %get-tuple-element.58), channel_id=1, source_target_pairs={{0,1},{1,0},{4,5},{5,4},{8,9},{9,8},{12,13},{13,12},{2,3},{3,2},{6... | collective-permute-start | bytes 786440 | tf_op jit(solution)/shard_map/ppermute | solution.py:497
  18.2 14.1 %collective-permute-start.3 = (f32[128,512]{1,0:T(8,128)S(1)}, f32[128,512]{1,0:T(8,128)S(1)}, u32[]{:S(2)}, u32[]{:S(2)}) collective-permute-start(f32[128,512]{1,0:T(8,128)S(1)} %get-tuple-element.66), channel_id=1, source_target_pairs={{0,5},{1,4},{4,1},{5,0},{8,13},{9,12},{12,9},{13,8},{2,7},{3,6},{6... | collective-permute-start | bytes 786440 | tf_op jit(solution)/shard_map/ppermute | solution.py:497
  20.2 18.3 %collective-permute-start.4 = (f32[128,512]{1,0:T(8,128)S(1)}, f32[128,512]{1,0:T(8,128)S(1)}, u32[]{:S(2)}, u32[]{:S(2)}) collective-permute-start(f32[128,512]{1,0:T(8,128)S(1)} %get-tuple-element.67), channel_id=1, source_target_pairs={{0,4},{1,5},{4,0},{5,1},{8,12},{9,13},{12,8},{13,9},{2,6},{3,7},{6... | collective-permute-start | bytes 786440 | tf_op jit(solution)/shard_map/ppermute | solution.py:497
  20.6 17.9 %collective-permute-start.5 = (f32[128,512]{1,0:T(8,128)S(1)}, f32[128,512]{1,0:T(8,128)S(1)}, u32[]{:S(2)}, u32[]{:S(2)}) collective-permute-start(f32[128,512]{1,0:T(8,128)S(1)} %get-tuple-element.68), channel_id=1, source_target_pairs={{0,1},{1,0},{4,5},{5,4},{8,9},{9,8},{12,13},{13,12},{2,3},{3,2},{6... | collective-permute-start | bytes 786440 | tf_op jit(solution)/shard_map/ppermute | solution.py:497
  21.6 20.1 %collective-permute-start.6 = (f32[264,256]{1,0:T(8,128)S(1)}, f32[264,256]{1,0:T(8,128)S(1)}, u32[]{:S(2)}, u32[]{:S(2)}) collective-permute-start(f32[264,256]{1,0:T(8,128)S(1)} %get-tuple-element.70.refs_0_), channel_id=1, source_target_pairs={{0,8},{1,9},{4,12},{5,13},{8,0},{9,1},{12,4},{13,5},{2,10},{3,11},... | collective-permute-start | bytes 811016 | tf_op jit(solution)/shard_map/ppermute | solution.py:504
  39.5 18.8 %collective-permute-start.7 = (f32[264,256]{1,0:T(8,128)S(1)}, f32[264,256]{1,0:T(8,128)S(1)}, u32[]{:S(2)}, u32[]{:S(2)}) collective-permute-start(f32[264,256]{1,0:T(8,128)S(1)} %get-tuple-element.72.refs_0_), channel_id=1, source_target_pairs={{0,8},{1,9},{4,12},{5,13},{8,0},{9,1},{12,4},{13,5},{2,10},{3,11},... | collective-permute-start | bytes 811016 | tf_op jit(solution)/shard_map/ppermute | solution.py:504
  55.5 15.3 %collective-permute-start.8 = (f32[512,256]{1,0:T(8,128)S(1)}, f32[512,256]{1,0:T(8,128)S(1)}, u32[]{:S(2)}, u32[]{:S(2)}) collective-permute-start(f32[512,256]{1,0:T(8,128)S(1)} %turn.5.refs_0_), channel_id=1, source_target_pairs={{1,0},{9,8},{4,1},{12,9},{5,4},{13,12},{7,5},{15,13},{6,7},{14,15}... | collective-permute-start | bytes 1572872 | tf_op jit(solution)/shard_map/ppermute | solution.py:519
  71.7 15.9 %collective-permute-start.11 = (f32[264,256]{1,0:T(8,128)S(1)}, f32[264,256]{1,0:T(8,128)S(1)}, u32[]{:S(2)}, u32[]{:S(2)}) collective-permute-start(f32[264,256]{1,0:T(8,128)S(1)} %get-tuple-element.88.refs_0_), channel_id=1, source_target_pairs={{0,8},{1,9},{4,12},{5,13},{8,0},{9,1},{12,4},{13,5},{2,10},{3,11},... | collective-permute-start | bytes 811016 | tf_op jit(solution)/shard_map/ppermute | solution.py:504
  73.6 14.0 %collective-permute-start.9 = (f32[256,256]{1,0:T(8,128)S(1)}, f32[256,256]{1,0:T(8,128)S(1)}, u32[]{:S(2)}, u32[]{:S(2)}) collective-permute-start(f32[256,256]{1,0:T(8,128)S(1)} %get-tuple-element.75), channel_id=1, source_target_pairs={{0,1},{8,9},{1,4},{9,12},{4,5},{12,13},{5,7},{13,15},{7,6},{15,14}... | collective-permute-start | bytes 786440 | tf_op jit(solution)/shard_map/ppermute | solution.py:519
  76.4 11.2 %collective-permute-start.10 = (f32[256,256]{1,0:T(8,128)S(1)}, f32[256,256]{1,0:T(8,128)S(1)}, u32[]{:S(2)}, u32[]{:S(2)}) collective-permute-start(f32[256,256]{1,0:T(8,128)S(1)} %get-tuple-element.76), channel_id=1, source_target_pairs={{0,1},{8,9},{1,4},{9,12},{4,5},{12,13},{5,7},{13,15},{7,6},{15,14}... | collective-permute-start | bytes 786440 | tf_op jit(solution)/shard_map/ppermute | solution.py:519
  88.8 23.0 %collective-permute-start.12 = (f32[264,256]{1,0:T(8,128)S(1)}, f32[264,256]{1,0:T(8,128)S(1)}, u32[]{:S(2)}, u32[]{:S(2)}) collective-permute-start(f32[264,256]{1,0:T(8,128)S(1)} %get-tuple-element.82.refs_0_), channel_id=1, source_target_pairs={{0,8},{1,9},{4,12},{5,13},{8,0},{9,1},{12,4},{13,5},{2,10},{3,11},... | collective-permute-start | bytes 811016 | tf_op jit(solution)/shard_map/ppermute | solution.py:504
  102.7 26.5 %collective-permute-start.16 = (f32[128,512]{1,0:T(8,128)S(1)}, f32[128,512]{1,0:T(8,128)S(1)}, u32[]{:S(2)}, u32[]{:S(2)}) collective-permute-start(f32[128,512]{1,0:T(8,128)S(1)} %get-tuple-element.90), channel_id=1, source_target_pairs={{0,5},{1,4},{4,1},{5,0},{8,13},{9,12},{12,9},{13,8},{2,7},{3,6},{6... | collective-permute-start | bytes 786440 | tf_op jit(solution)/shard_map/ppermute | solution.py:497
  104.7 24.5 %collective-permute-start.17 = (f32[128,512]{1,0:T(8,128)S(1)}, f32[128,512]{1,0:T(8,128)S(1)}, u32[]{:S(2)}, u32[]{:S(2)}) collective-permute-start(f32[128,512]{1,0:T(8,128)S(1)} %get-tuple-element.91), channel_id=1, source_target_pairs={{0,4},{1,5},{4,0},{5,1},{8,12},{9,13},{12,8},{13,9},{2,6},{3,7},{6... | collective-permute-start | bytes 786440 | tf_op jit(solution)/shard_map/ppermute | solution.py:497
  111.7 17.6 %collective-permute-start.18 = (f32[128,512]{1,0:T(8,128)S(1)}, f32[128,512]{1,0:T(8,128)S(1)}, u32[]{:S(2)}, u32[]{:S(2)}) collective-permute-start(f32[128,512]{1,0:T(8,128)S(1)} %get-tuple-element.92), channel_id=1, source_target_pairs={{0,1},{1,0},{4,5},{5,4},{8,9},{9,8},{12,13},{13,12},{2,3},{3,2},{6... | collective-permute-start | bytes 786440 | tf_op jit(solution)/shard_map/ppermute | solution.py:497
  125.6 8.1 %collective-permute-start.13 = (f32[128,512]{1,0:T(8,128)S(1)}, f32[128,512]{1,0:T(8,128)S(1)}, u32[]{:S(2)}, u32[]{:S(2)}) collective-permute-start(f32[128,512]{1,0:T(8,128)S(1)} %get-tuple-element.84), channel_id=1, source_target_pairs={{0,5},{1,4},{4,1},{5,0},{8,13},{9,12},{12,9},{13,8},{2,7},{3,6},{6... | collective-permute-start | bytes 786440 | tf_op jit(solution)/shard_map/ppermute | solution.py:497
  128.4 11.5 %collective-permute-start.14 = (f32[128,512]{1,0:T(8,128)S(1)}, f32[128,512]{1,0:T(8,128)S(1)}, u32[]{:S(2)}, u32[]{:S(2)}) collective-permute-start(f32[128,512]{1,0:T(8,128)S(1)} %get-tuple-element.85), channel_id=1, source_target_pairs={{0,4},{1,5},{4,0},{5,1},{8,12},{9,13},{12,8},{13,9},{2,6},{3,7},{6... | collective-permute-start | bytes 786440 | tf_op jit(solution)/shard_map/ppermute | solution.py:497
  129.2 10.7 %collective-permute-start.15 = (f32[128,512]{1,0:T(8,128)S(1)}, f32[128,512]{1,0:T(8,128)S(1)}, u32[]{:S(2)}, u32[]{:S(2)}) collective-permute-start(f32[128,512]{1,0:T(8,128)S(1)} %get-tuple-element.86), channel_id=1, source_target_pairs={{0,1},{1,0},{4,5},{5,4},{8,9},{9,8},{12,13},{13,12},{2,3},{3,2},{6... | collective-permute-start | bytes 786440 | tf_op jit(solution)/shard_map/ppermute | solution.py:497
where the time goes:
time: 142 us
  Pallas kernels  69.8 us (49%)
  waiting for transfers between devices  42.3 us (30%)
  starting transfers between devices  29.3 us (21%)
    pallas_call x4, Pallas kernels, factor(): call(factor_kernel, 'factor', f32(2, BLK, 2 * BLK), [VMEM_SPEC] * len(ter...  49.8 us
    ppermute x12, waiting for transfers between devices, exchange(): arrived.append(lax.ppermute(piece, token_axes, route))  35.9 us
    ppermute x12, starting transfers between devices, exchange(): arrived.append(lax.ppermute(piece, token_axes, route))  15.5 us
    ppermute x3, starting transfers between devices, along(): return lax.ppermute(block, all_axes, route)  7.76 us
    ppermute x4, waiting for transfers between devices, shared(): gathered.append(lax.ppermute(terms, token_axes, route))  6.36 us
    ppermute x4, starting transfers between devices, shared(): gathered.append(lax.ppermute(terms, token_axes, route))  5.95 us
    pallas_call x4, Pallas kernels, turn_out(): call(functools.partial(turn_out_kernel, layout, partners), 'turn_out', [f...  5.49 us
    pallas_call x4, Pallas kernels, turn(): call(functools.partial(turn_kernel, m), 'turn', [f32(blocks.shape[1] // p...  5.05 us
  transfers between devices with their start and end apart: 19, of which 7 were waited for; matrix products, arithmetic and copies ran while one was open for 0% of the time, Pallas kernels for 45%

commit v1 on v0

--- a/solution.py
+++ b/solution.py
@@ -36,6 +36,28 @@
 def reciprocal(x):
     guess = pl.reciprocal(x, approx=True)
     return guess, 2.0 - x * guess
+
+
+def split(x):
+    high = x.astype(jnp.bfloat16).astype(jnp.float32)
+    rest = x - high
+    middle = rest.astype(jnp.bfloat16).astype(jnp.float32)
+    return high, middle, rest - middle
+
+
+def packed_product(doubled, rows):
+    high, middle, low = split(doubled)
+    mixed = jnp.where(iota2(doubled.shape, 1) < PANEL, high, low)
+    left = jnp.concatenate([part.astype(jnp.bfloat16) for part in (high, middle, mixed)], axis=1)
+    high, middle, low = (part.astype(jnp.bfloat16) for part in split(rows))
+    right = jnp.concatenate([high, middle, high, middle, low, high], axis=0)
+    return lax.dot_general(
+        left, right, (((1,), (0,)), ((), ())), preferred_element_type=jnp.float32
+    )
+
+
+def doubled_transpose(x):
+    return jnp.transpose(jnp.concatenate([x, x], axis=0))
 
 
 def eliminate(blocks):
@@ -93,10 +115,12 @@
             tile = jnp.where(sub == i, side_rows[i] * lax.rsqrt(entry[i][i]), tile)
         outs.append(tile)
     out = jnp.concatenate(outs, axis=0)
-    return out[:, :PANEL], out[:, PANEL:]
-
-
-def inverse_factors(work_ref):
+    turned_out = pltpu.roll(out, PANEL, 1)
+    left = iota2(out.shape, 1) < PANEL
+    return jnp.where(left, out, turned_out), jnp.where(left, turned_out, out)
+
+
+def half_step(work_ref, h):
     lane = iota2((PANEL, BLK), 1)
     line = iota2((PANEL, BLK), 0)
     first_ident = jnp.where(line == lane, 1.0, 0.0).astype(jnp.float32)
@@ -105,41 +129,41 @@
     own = lane < HALF
     second_own = jnp.logical_and(own, lane >= PANEL)
     lane_below = iota2((HALF, BLK), 1)
-    first_own_below = lane_below < PANEL
-    own_below = lane_below < HALF
-
-    def step(h, _):
-        waiting = jnp.full((PANEL, BLK), h, jnp.int32) == 0
-        over = jnp.logical_not(waiting)
-        panels = [jnp.concatenate([work_ref[m, h, h], work_ref[m, h, 1 - h]], axis=1) for m in range(2)]
-        belows = [
-            jnp.concatenate([work_ref[m, 1 - h, h], work_ref[m, 1 - h, 1 - h]], axis=1)
-            for m in range(2)
-        ]
-        invs = eliminate([panel[:PANEL, :PANEL] for panel in panels])
-        tops, seconds = [], []
-        for m in range(2):
-            rows = contract(invs[m], jnp.where(first_own, first_ident, panels[m][:PANEL]), 1, 0)
-            factors = jnp.where(jnp.logical_or(own, waiting), rows, 0.0)
-            change = contract(factors[:, PANEL:], rows, 0, 0)
-            seconds.append(jnp.where(first_own, 0.0, panels[m][PANEL:]) - change[:PANEL])
-            belows[m] = jnp.where(first_own_below, 0.0, belows[m]) - change[PANEL:]
-            keep = jnp.logical_or(first_own, jnp.logical_and(jnp.logical_not(own), over))
-            tops.append(jnp.where(keep, rows, 0.0))
-        invs = eliminate([second[:, PANEL:HALF] for second in seconds])
-        for m in range(2):
-            rows = contract(invs[m], jnp.where(second_own, second_ident, seconds[m]), 1, 0)
-            factors = jnp.where(waiting, rows, 0.0)
-            change = contract(factors[:, HALF:], rows, 0, 0)
-            below = jnp.where(own_below, jnp.where(first_own_below, belows[m], 0.0), belows[m]) - change
-            done = jnp.concatenate([tops[m], jnp.where(jnp.logical_or(own, over), rows, 0.0)], axis=0)
-            work_ref[m, h, h] = done[:, :HALF]
-            work_ref[m, h, 1 - h] = done[:, HALF:]
-            work_ref[m, 1 - h, h] = below[:, :HALF]
-            work_ref[m, 1 - h, 1 - h] = below[:, HALF:]
-        return 0
-
-    lax.fori_loop(0, 2, step, 0)
+    other = 1 - h
+    known = isinstance(h, int)
+    others_rows = not known or h == 0
+    over = jnp.full((PANEL, BLK), h, jnp.int32) == 1
+
+    def for_others(rows):
+        return rows if known else jnp.where(jnp.logical_or(own, jnp.logical_not(over)), rows, 0.0)
+
+    panels = [jnp.concatenate([work_ref[m, h, h], work_ref[m, h, other]], axis=1) for m in range(2)]
+    invs = eliminate([panel[:PANEL, :PANEL] for panel in panels])
+    tops, seconds, belows = [], [], []
+    for m in range(2):
+        rows = packed_product(invs[m], jnp.where(first_own, first_ident, panels[m][:PANEL]))
+        factors = for_others(rows) if others_rows else rows[:, :HALF]
+        change = packed_product(doubled_transpose(factors)[PANEL:], rows)
+        seconds.append(jnp.where(first_own, 0.0, panels[m][PANEL:]) - change[:PANEL])
+        if others_rows:
+            below = jnp.concatenate([work_ref[m, other, h], work_ref[m, other, other]], axis=1)
+            belows.append(jnp.where(lane_below < PANEL, 0.0, below) - change[PANEL:])
+        keep = jnp.logical_or(first_own, jnp.logical_and(over, jnp.logical_not(own)))
+        tops.append(jnp.where(keep, rows, 0.0))
+    invs = eliminate([second[:, PANEL:HALF] for second in seconds])
+    for m in range(2):
+        rows = packed_product(invs[m], jnp.where(second_own, second_ident, seconds[m]))
+        if others_rows:
+            factors = for_others(rows)[:, HALF:]
+            change = packed_product(doubled_transpose(factors), rows)
+            gone = jnp.logical_and(lane_below >= PANEL, lane_below < HALF)
+            below = jnp.where(gone, 0.0, belows[m]) - change
+            work_ref[m, other, h] = below[:, :HALF]
+            work_ref[m, other, other] = below[:, HALF:]
+        rows = jnp.where(jnp.logical_or(own, over), rows, 0.0)
+        done = jnp.concatenate([tops[m], rows], axis=0)
+        work_ref[m, h, h] = done[:, :HALF]
+        work_ref[m, h, other] = done[:, HALF:]
 
 
 def pair_terms(blocks_ref, terms_ref):
@@ -322,21 +346,9 @@
     inputs, (blocks_ref, terms_ref) = refs[:-2], refs[-2:]
 
     def fetch(m, at):
-        refs = [inputs[i] for i in at]
-        if len(refs[0].shape) == 3:
-            pair_ref, inv_ref = refs
-            chunk = min(CHUNK, pair_ref.shape[1])
-
-            def step(i, _):
-                rows = pl.ds(pl.multiple_of(i * chunk, chunk), chunk)
-                blocks_ref[m, rows, :] = turned(pair_ref[0, rows, :], pair_ref[1, rows, :], inv_ref, 0)
-                return 0
-
-            lax.fori_loop(0, pair_ref.shape[1] // chunk, step, 0)
-        else:
-            rows = refs[0].shape[0]
-            for i, ref in enumerate(refs):
-                blocks_ref[m, i * rows : (i + 1) * rows, :] = ref[...]
+        rows = inputs[at[0]].shape[0]
+        for i, place in enumerate(at):
+            blocks_ref[m, i * rows : (i + 1) * rows, :] = inputs[place][...]
 
     for m, (pick, choices) in enumerate(((pick_upper, uppers), (pick_lower, lowers))):
         chosen = pick()
@@ -362,6 +374,37 @@
     )(*inputs)
 
 
+def edge_terms_kernel(layout, pair_ref, inv_ref, old_blocks_ref, old_terms_ref, blocks_ref, terms_ref):
+    chunk = min(CHUNK, pair_ref.shape[1])
+    blocks_ref[...] = old_blocks_ref[...]
+
+    def step(i, _):
+        rows = pl.ds(pl.multiple_of(i * chunk, chunk), chunk)
+        blocks_ref[1, rows, :] = turned(pair_ref[0, rows, :], pair_ref[1, rows, :], inv_ref, 0)
+        return 0
+
+    @pl.when(layout.final())
+    def _():
+        lax.fori_loop(0, pair_ref.shape[1] // chunk, step, 0)
+        pair_terms(blocks_ref, terms_ref)
+
+    @pl.when(jnp.logical_not(layout.final()))
+    def _():
+        terms_ref[...] = old_terms_ref[...]
+
+
+def edge_terms(layout, pair, factors, blocks, terms):
+    return call(
+        functools.partial(edge_terms_kernel, layout),
+        "edge_terms",
+        [f32(*blocks.shape), f32(*terms.shape)],
+        [VMEM_SPEC] * 4,
+        [VMEM_SPEC] * 2,
+        [],
+        1,
+    )(pair, factors, blocks, terms)
+
+
 def total_terms(refs):
     total = refs[0][...]
     for ref in refs[1:]:
@@ -369,11 +412,10 @@
     return total
 
 
-def factor_kernel(*refs):
-    terms, (inv_ref, corr_ref, work_ref) = refs[:-3], refs[-3:]
-    terms = total_terms(terms)
+def start_factor(terms, corr_ref, work_ref):
     square = (BLK, BLK)
     diagonal = iota2(square, 0) == iota2(square, 1)
+    ident = jnp.where(diagonal, 1.0, 0.0).astype(jnp.float32)
     upper_sq, lower_sq = terms[BLK : BLK + 1], terms[BLK + 1 : BLK + 2]
     upper_sq = jnp.sum(
         jnp.where(diagonal, jnp.broadcast_to(upper_sq, square), 0.0), axis=1, keepdims=True
@@ -381,27 +423,37 @@
     corr = terms[:BLK] * lax.rsqrt(upper_sq + epsilon) * lax.rsqrt(lower_sq + epsilon)
     corr_ref[0] = corr
     corr_ref[1] = -jnp.transpose(corr)
-
-    def gram(m, _):
-        corr = corr_ref[m]
-        whole = jnp.where(diagonal, 1.0, 0.0).astype(jnp.float32) + contract(corr, corr, 1, 1)
+    for m in range(2):
+        whole = ident + contract(corr_ref[m], corr_ref[m], 1, 1)
         for r in range(2):
             for c in range(2):
                 work_ref[m, r, c] = whole[HALF * r : HALF * (r + 1), HALF * c : HALF * (c + 1)]
-        return 0
-
-    def widen(m, _):
+
+
+def finish_factor(corr_ref, work_ref, inv_ref):
+    for m in range(2):
         whole = jnp.concatenate(
             [jnp.concatenate([work_ref[m, r, 0], work_ref[m, r, 1]], axis=1) for r in range(2)],
             axis=0,
         )
         inv_ref[m, :, :BLK] = whole
         inv_ref[m, :, BLK:] = contract(whole, corr_ref[m], 1, 0)
+
+
+CORR_SHAPE = (2, BLK, BLK)
+WORK_SHAPE = (2, 2, 2, HALF, HALF)
+
+
+def factor_kernel(*refs):
+    terms, (inv_ref, corr_ref, work_ref) = refs[:-3], refs[-3:]
+    start_factor(total_terms(terms), corr_ref, work_ref)
+
+    def step(h, _):
+        half_step(work_ref, h)
         return 0
 
-    lax.fori_loop(0, 2, gram, 0)
-    inverse_factors(work_ref)
-    lax.fori_loop(0, 2, widen, 0)
+    lax.fori_loop(0, 2, step, 0)
+    finish_factor(corr_ref, work_ref, inv_ref)
 
 
 def factor(terms):
@@ -411,12 +463,45 @@
         f32(2, BLK, 2 * BLK),
         [VMEM_SPEC] * len(terms),
         VMEM_SPEC,
-        [
-            pltpu.VMEM((2, BLK, BLK), jnp.float32),
-            pltpu.VMEM((2, 2, 2, HALF, HALF), jnp.float32),
-        ],
+        [pltpu.VMEM(CORR_SHAPE, jnp.float32), pltpu.VMEM(WORK_SHAPE, jnp.float32)],
         11,
     )(*terms)
+
+
+def factor_start_kernel(*refs):
+    terms, (corr_ref, work_ref) = refs[:-2], refs[-2:]
+    start_factor(total_terms(terms), corr_ref, work_ref)
+    half_step(work_ref, 0)
+
+
+def factor_start(terms):
+    return call(
+        factor_start_kernel,
+        "factor_start",
+        [f32(*CORR_SHAPE), f32(*WORK_SHAPE)],
+        [VMEM_SPEC] * len(terms),
+        [VMEM_SPEC] * 2,
+        [],
+        6,
+    )(*terms)
+
+
+def factor_finish_kernel(corr_ref, held_ref, inv_ref, work_ref):
+    work_ref[...] = held_ref[...]
+    half_step(work_ref, 1)
+    finish_factor(corr_ref, work_ref, inv_ref)
+
+
+def factor_finish(corr, work):
+    return call(
+        factor_finish_kernel,
+        "factor_finish",
+        f32(2, BLK, 2 * BLK),
+        [VMEM_SPEC] * 2,
+        VMEM_SPEC,
+        [pltpu.VMEM(WORK_SHAPE, jnp.float32)],
+        5,
+    )(corr, work)
 
 
 def turned(own, other, inv_ref, m):
@@ -497,11 +582,21 @@
             arrived.append(lax.ppermute(piece, token_axes, route))
         return arrived
 
-    def shared(terms):
-        gathered = [terms]
+    def position(at, group):
+        home, inner = divmod(at, team)
+        inner = team - 1 - inner if home % 2 else inner
+        row, sub = divmod(group * team + inner, subs)
+        return (row * columns + home) * subs + sub
+
+    def shared(terms, places=range(columns * team)):
+        gathered = []
         for step in range(1, teams):
-            route = [(t, (t + step * team) % token_group) for t in range(token_group)]
-            gathered.append(lax.ppermute(terms, token_axes, route))
+            route = [
+                (position(at, group), position(at, (group + step) % teams))
+                for at in places
+                for group in range(teams)
+            ]
+            gathered.append(lax.ppermute(terms, all_axes, route))
         return gathered
 
     def along(block, distance):
@@ -509,13 +604,7 @@
         for at in range(columns * team):
             if 0 <= at + distance < columns * team:
                 for group in range(teams):
-                    ends = []
-                    for one in (at, at + distance):
-                        home, inner = divmod(one, team)
-                        inner = team - 1 - inner if home % 2 else inner
-                        row, sub = divmod(group * team + inner, subs)
-                        ends.append((row * columns + home) * subs + sub)
-                    route.append(tuple(ends))
+                    route.append((position(at, group), position(at + distance, group)))
         return lax.ppermute(block, all_axes, route)
 
     def always():
@@ -534,10 +623,10 @@
             piece, arrived[-1] = lax.optimization_barrier((piece, arrived[-1]))
         arrived.append(exchange(piece))
     ready = [gather_terms(layout, piece) for piece in arrived]
-    summed = [shared(terms) for _, terms in ready]
+    summed = [[terms] + shared(terms) for _, terms in ready]
     top = held - 1
 
-    def next_terms(g, uppers, lowers, edge, leaving, arriving):
+    def next_blocks(g, uppers, lowers, edge, leaving, arriving):
         if g == 0:
             from_above, pick_upper = (uppers[0], arriving), layout.first
         elif g == 1:
@@ -548,8 +637,7 @@
             from_below, pick_lower = (edge, leaving), layout.final
         else:
             from_below, pick_lower = (lowers[g + 1],) * 2, always
-        blocks, terms = choose_terms((pick_upper, pick_lower), from_above, from_below)
-        return blocks, shared(terms)
+        return choose_terms((pick_upper, pick_lower), from_above, from_below)
 
     for g in range(1, held):
         summed[0][0], summed[g][0] = lax.optimization_barrier((summed[0][0], summed[g][0]))
@@ -561,17 +649,26 @@
         if g == 0:
             leaving = [along(part, -1) for part in lowers[0]]
         uppers[g] = turn(0, ready[g][0], factors)
-    factors = factor(summed[top])
     if top:
-        nexts[top] = next_terms(top, uppers, lowers, [ready[top][0], factors], leaving, None)
-        factors, nexts[top][1][0] = lax.optimization_barrier((factors, nexts[top][1][0]))
-    uppers[top] = turn(0, ready[top][0], factors, UP_PARTS)
-    if top:
+        corr, work = factor_start(summed[top])
+        work, leaving = lax.optimization_barrier((work, leaving))
+        blocks, terms = next_blocks(top, uppers, lowers, leaving, leaving, None)
+        end = columns * team - 1
+        early = shared(terms, range(end))
+        work, terms = lax.optimization_barrier((work, terms))
+        factors = factor_finish(corr, work)
+        blocks, terms = edge_terms(layout, ready[top][0], factors, blocks, terms)
+        late = shared(terms, [end])
+        nexts[top] = (blocks, [terms] + early + late)
+        factors, terms = lax.optimization_barrier((factors, terms))
+        uppers[top] = turn(0, ready[top][0], factors, UP_PARTS)
         arriving = [along(part, 1) for part in uppers[top]]
         lowers[top] = turn(1, ready[top][0], factors)
-        for term in nexts[top][1]:
+        for term in early + late:
             lowers[top][0], term = lax.optimization_barrier((lowers[top][0], term))
     else:
+        factors = factor(summed[0])
+        uppers[0] = turn(0, ready[0][0], factors, UP_PARTS)
         lowers[0] = turn(1, ready[0][0], factors, UP_PARTS)
         arriving = [
             along(jnp.where(layout.first(), low, up), 1) for low, up in zip(lowers[0], uppers[0])
@@ -579,7 +676,8 @@
         leaving = [along(part, -1) for part in lowers[0]]
     for g in reversed(range(held)):
         if nexts[g] is None:
-            nexts[g] = next_terms(g, uppers, lowers, uppers[top], leaving, arriving)
+            blocks, terms = next_blocks(g, uppers, lowers, uppers[top], leaving, arriving)
+            nexts[g] = (blocks, [terms] + shared(terms))
 
     for g in range(1, held):
         nexts[0][1][0], nexts[g][1][0] = lax.optimization_barrier((nexts[0][1][0], nexts[g][1][0]))

time: 142 us -> 134 us (0.944)
  waiting for transfers between devices: 42.3 us -> 35.9 us
  Pallas kernels: 69.8 us -> 64.3 us
  starting transfers between devices: 29.3 us -> 32.7 us
    pallas_call x4 -> x3, Pallas kernels: 49.8 us -> 33.5 us  [factor(): call(factor_kernel, 'factor', f32(2, BLK, 2 * BLK), [VMEM_SPEC] * len(ter...]
    pallas_call x0 -> x3, Pallas kernels: none -> 10.7 us  [the longest x1 5.57 us: factor_start(): call(factor_start_kernel, 'factor_start', [f32(*CORR_SHAPE), f32(*WORK_SH...]
    ppermute x4 -> x5, waiting for transfers between devices: 6.36 us -> 0.01 us  [shared(): gathered.append(lax.ppermute(terms, all_axes, route))]
    ppermute x4 -> x5, starting transfers between devices: 5.95 us -> 11.4 us  [shared(): gathered.append(lax.ppermute(terms, all_axes, route))]
    ppermute x12, starting transfers between devices: 15.5 us -> 13.8 us  [exchange(): arrived.append(lax.ppermute(piece, token_axes, route))]
  transfers between devices with their start and end apart: 19 -> 20, of which waited for: 7 -> 6; matrix products, arithmetic and copies ran while one was open for 0% -> 0% of each run, Pallas kernels for 45% -> 43%
where the time goes in v1:
time: 134 us; the launch traced here: 133 us
  Pallas kernels  64.3 us (48%)
  waiting for transfers between devices  35.9 us (27%)
  starting transfers between devices  32.7 us (24%)
    ppermute x12, waiting for transfers between devices, exchange(): arrived.append(lax.ppermute(piece, token_axes, route))  35.9 us
    pallas_call x3, Pallas kernels, factor(): call(factor_kernel, 'factor', f32(2, BLK, 2 * BLK), [VMEM_SPEC] * len(ter...  33.5 us
    ppermute x12, starting transfers between devices, exchange(): arrived.append(lax.ppermute(piece, token_axes, route))  13.8 us
    ppermute x5, starting transfers between devices, shared(): gathered.append(lax.ppermute(terms, all_axes, route))  11.4 us
    ppermute x3, starting transfers between devices, along(): return lax.ppermute(block, all_axes, route)  7.52 us
    pallas_call x1, Pallas kernels, factor_start(): call(factor_start_kernel, 'factor_start', [f32(*CORR_SHAPE), f32(*WORK_SH...  5.57 us
    pallas_call x4, Pallas kernels, turn_out(): call(functools.partial(turn_out_kernel, layout, partners), 'turn_out', [f...  5.48 us
    pallas_call x1, Pallas kernels, factor_finish(): call(factor_finish_kernel, 'factor_finish', f32(2, BLK, 2 * BLK), [VMEM_S...  5.01 us
  transfers between devices with their start and end apart: 20, of which 6 were waited for; matrix products, arithmetic and copies ran while one was open for 0% of the time, Pallas kernels for 43%

profile of v1, /device:TPU:0, one launch (start us, length us, event | category | flops | bytes accessed | tf_op | source)
XLA Modules:
  0.0 133.4 jit_solution(18323470925078165399)
XLA Ops:
  0.0 3.0 %pack.2 = (f32[128,512]{1,0:T(8,128)}, f32[128,512]{1,0:T(8,128)}, f32[128,512]{1,0:T(8,128)}) custom-call(s32[2,32]{1,0:T(2,128)} %plan_ref.2, f32[128,4096]{1,0:T(8,128)} %x_ref.3), custom_call_target="tpu_custom_call" | custom-call | flops 2000000000 | bytes 1048576 | tf_op jit(solution)/shard_map/pack/pallas_call | solution.py:273
  3.0 2.5 %collective-permute-start = (f32[128,512]{1,0:T(8,128)}, f32[128,512]{1,0:T(8,128)S(1)}, u32[]{:S(2)}, u32[]{:S(2)}) collective-permute-start(f32[128,512]{1,0:T(8,128)} %get-tuple-element.63), channel_id=1, source_target_pairs={{0,5},{1,4},{4,1},{5,0},{8,13},{9,12},{12,9},{13,8},{2,7},{3,6},{6... | collective-permute-start | bytes 786440 | tf_op jit(solution)/shard_map/ppermute | solution.py:582
  7.1 5.4 %collective-permute-done.refs_1_ = f32[128,512]{1,0:T(8,128)S(1)} collective-permute-done((f32[128,512]{1,0:T(8,128)}, f32[128,512]{1,0:T(8,128)S(1)}, u32[]{:S(2)}, u32[]{:S(2)}) %collective-permute-start) | collective-permute-done | bytes 262176 | tf_op jit(solution)/shard_map/ppermute | solution.py:582
  12.5 5.7 %collective-permute-done.1.refs_2_ = f32[128,512]{1,0:T(8,128)S(1)} collective-permute-done((f32[128,512]{1,0:T(8,128)}, f32[128,512]{1,0:T(8,128)S(1)}, u32[]{:S(2)}, u32[]{:S(2)}) %collective-permute-start.1) | collective-permute-done | bytes 262176 | tf_op jit(solution)/shard_map/ppermute | solution.py:582
  18.2 2.0 %collective-permute-start.3 = (f32[128,512]{1,0:T(8,128)S(1)}, f32[128,512]{1,0:T(8,128)S(1)}, u32[]{:S(2)}, u32[]{:S(2)}) collective-permute-start(f32[128,512]{1,0:T(8,128)S(1)} %get-tuple-element.73), channel_id=1, source_target_pairs={{0,5},{1,4},{4,1},{5,0},{8,13},{9,12},{12,9},{13,8},{2,7},{3,6},{6... | collective-permute-start | bytes 786440 | tf_op jit(solution)/shard_map/ppermute | solution.py:582
  21.6 2.8 %collective-permute-start.6 = (f32[264,256]{1,0:T(8,128)S(1)}, f32[264,256]{1,0:T(8,128)S(1)}, u32[]{:S(2)}, u32[]{:S(2)}) collective-permute-start(f32[264,256]{1,0:T(8,128)S(1)} %get-tuple-element.77.refs_0_), channel_id=1, source_target_pairs={{0,8},{8,0},{1,9},{9,1},{4,12},{12,4},{5,13},{13,5},{7,15},{15,7},... | collective-permute-start | bytes 811016 | tf_op jit(solution)/shard_map/ppermute | solution.py:599
  24.4 7.9 %collective-permute-done.3.refs_1_ = f32[128,512]{1,0:T(8,128)S(1)} collective-permute-done((f32[128,512]{1,0:T(8,128)S(1)}, f32[128,512]{1,0:T(8,128)S(1)}, u32[]{:S(2)}, u32[]{:S(2)}) %collective-permute-start.3) | collective-permute-done | bytes 262176 | tf_op jit(solution)/shard_map/ppermute | solution.py:582
  32.3 6.1 %collective-permute-done.4.refs_2_ = f32[128,512]{1,0:T(8,128)S(1)} collective-permute-done((f32[128,512]{1,0:T(8,128)S(1)}, f32[128,512]{1,0:T(8,128)S(1)}, u32[]{:S(2)}, u32[]{:S(2)}) %collective-permute-start.4) | collective-permute-done | bytes 262176 | tf_op jit(solution)/shard_map/ppermute | solution.py:582
  39.4 2.2 %collective-permute-start.7 = (f32[264,256]{1,0:T(8,128)S(1)}, f32[264,256]{1,0:T(8,128)S(1)}, u32[]{:S(2)}, u32[]{:S(2)}) collective-permute-start(f32[264,256]{1,0:T(8,128)S(1)} %get-tuple-element.79.refs_0_), channel_id=1, source_target_pairs={{0,8},{8,0},{1,9},{9,1},{4,12},{12,4},{5,13},{13,5},{7,15},{15,7},... | collective-permute-start | bytes 811016 | tf_op jit(solution)/shard_map/ppermute | solution.py:599
  41.7 11.2 %factor.3.inv_ref = f32[2,256,512]{2,1,0:T(8,128)S(1)} custom-call(f32[264,256]{1,0:T(8,128)S(1)} %get-tuple-element.77.refs_0_, f32[264,256]{1,0:T(8,128)S(1)} %collective-permute-done.6.refs_1_), custom_call_target="tpu_custom_call" | custom-call | flops 11000000512 | bytes 1048576 | tf_op jit(solution)/shard_map/factor/pallas_call | solution.py:460
  56.8 5.6 %factor_start.1 = (f32[2,256,256]{2,1,0:T(8,128)S(1)}, f32[2,2,2,128,128]{4,3,2,1,0:T(8,128)S(1)}) custom-call(f32[264,256]{1,0:T(8,128)S(1)} %get-tuple-element.79.refs_0_, f32[264,256]{1,0:T(8,128)S(1)} %collective-permute-done.7.refs_1_), custom_call_target="tpu_custom_call" | custom-call | flops 6000000000 | bytes 1048576 | tf_op jit(solution)/shard_map/factor_start/pallas_call | solution.py:478
  63.6 2.7 %collective-permute-start.11 = (f32[264,256]{1,0:T(8,128)S(1)}, f32[264,256]{1,0:T(8,128)S(1)}, u32[]{:S(2)}, u32[]{:S(2)}) collective-permute-start(f32[264,256]{1,0:T(8,128)S(1)} %get-tuple-element.87.old_terms_ref), channel_id=1, source_target_pairs={{0,8},{8,0},{1,9},{9,1},{4,12},{12,4},{5,13},{13,5},{7,15},{15,7},... | collective-permute-start | bytes 811016 | tf_op jit(solution)/shard_map/ppermute | solution.py:599
  66.3 5.0 %factor_finish.1.inv_ref = f32[2,256,512]{2,1,0:T(8,128)S(1)} custom-call(f32[2,256,256]{2,1,0:T(8,128)S(1)} %get-tuple-element.80.corr_ref, f32[2,2,2,128,128]{4,3,2,1,0:T(8,128)S(1)} %get-tuple-element.85.held_ref), custom_call_target="tpu_custom_call" | custom-call | flops 5000000000 | bytes 1048576 | tf_op jit(solution)/shard_map/factor_finish/pallas_call | solution.py:496
  73.1 4.2 %collective-permute-start.9 = (f32[256,256]{1,0:T(8,128)S(1)}, f32[256,256]{1,0:T(8,128)S(1)}, u32[]{:S(2)}, u32[]{:S(2)}) collective-permute-start(f32[256,256]{1,0:T(8,128)S(1)} %get-tuple-element.90), channel_id=1, source_target_pairs={{0,1},{8,9},{1,4},{9,12},{4,5},{12,13},{5,7},{13,15},{7,6},{15,14}... | collective-permute-start | bytes 786440 | tf_op jit(solution)/shard_map/ppermute | solution.py:608
  77.3 2.0 %collective-permute-start.10 = (f32[256,256]{1,0:T(8,128)S(1)}, f32[256,256]{1,0:T(8,128)S(1)}, u32[]{:S(2)}, u32[]{:S(2)}) collective-permute-start(f32[256,256]{1,0:T(8,128)S(1)} %get-tuple-element.91), channel_id=1, source_target_pairs={{0,1},{8,9},{1,4},{9,12},{4,5},{12,13},{5,7},{13,15},{7,6},{15,14}... | collective-permute-start | bytes 786440 | tf_op jit(solution)/shard_map/ppermute | solution.py:608
  81.9 3.0 %collective-permute-start.13 = (f32[264,256]{1,0:T(8,128)S(1)}, f32[264,256]{1,0:T(8,128)S(1)}, u32[]{:S(2)}, u32[]{:S(2)}) collective-permute-start(f32[264,256]{1,0:T(8,128)S(1)} %get-tuple-element.96.refs_0_), channel_id=1, source_target_pairs={{0,8},{8,0},{1,9},{9,1},{4,12},{12,4},{5,13},{13,5},{7,15},{15,7},... | collective-permute-start | bytes 811016 | tf_op jit(solution)/shard_map/ppermute | solution.py:599
  84.9 11.2 %factor.5.inv_ref = f32[2,256,512]{2,1,0:T(8,128)S(1)} custom-call(f32[264,256]{1,0:T(8,128)S(1)} %get-tuple-element.102.refs_0_, f32[264,256]{1,0:T(8,128)S(1)} %collective-permute-done.11.refs_1_, f32[264,256]{1,0:T(8,128)S(1)} %collective-permute-done.12.refs_2_), custom_call_target="tpu_custom_call" | custom-call | flops 11000000512 | bytes 1048576 | tf_op jit(solution)/shard_map/factor/pallas_call | solution.py:460
  97.4 4.5 %collective-permute-start.17 = (f32[128,512]{1,0:T(8,128)S(1)}, f32[128,512]{1,0:T(8,128)S(1)}, u32[]{:S(2)}, u32[]{:S(2)}) collective-permute-start(f32[128,512]{1,0:T(8,128)S(1)} %get-tuple-element.104), channel_id=1, source_target_pairs={{0,5},{1,4},{4,1},{5,0},{8,13},{9,12},{12,9},{13,8},{2,7},{3,6},{6... | collective-permute-start | bytes 786440 | tf_op jit(solution)/shard_map/ppermute | solution.py:582
  104.8 11.2 %factor.4.inv_ref = f32[2,256,512]{2,1,0:T(8,128)S(1)} custom-call(f32[264,256]{1,0:T(8,128)S(1)} %get-tuple-element.96.refs_0_, f32[264,256]{1,0:T(8,128)S(1)} %collective-permute-done.13.refs_1_), custom_call_target="tpu_custom_call" | custom-call | flops 11000000512 | bytes 1048576 | tf_op jit(solution)/shard_map/factor/pallas_call | solution.py:460
  115.9 1.4 %turn_out.5 = (f32[128,512]{1,0:T(8,128)S(1)}, f32[128,512]{1,0:T(8,128)S(1)}) custom-call(f32[2,512,256]{2,1,0:T(8,128)S(1)} %get-tuple-element.94.blocks_ref, f32[2,256,512]{2,1,0:T(8,128)S(1)} %factor.4.inv_ref), custom_call_target="tpu_custom_call" | custom-call | flops 2000000000 | bytes 1048576 | tf_op jit(solution)/shard_map/turn_out/pallas_call | solution.py:560
  117.3 1.4 %collective-permute-start.14 = (f32[128,512]{1,0:T(8,128)S(1)}, f32[128,512]{1,0:T(8,128)S(1)}, u32[]{:S(2)}, u32[]{:S(2)}) collective-permute-start(f32[128,512]{1,0:T(8,128)S(1)} %get-tuple-element.98), channel_id=1, source_target_pairs={{0,5},{1,4},{4,1},{5,0},{8,13},{9,12},{12,9},{13,8},{2,7},{3,6},{6... | collective-permute-start | bytes 786440 | tf_op jit(solution)/shard_map/ppermute | solution.py:582
  120.9 4.5 %collective-permute-done.14.refs_1_ = f32[128,512]{1,0:T(8,128)S(1)} collective-permute-done((f32[128,512]{1,0:T(8,128)S(1)}, f32[128,512]{1,0:T(8,128)S(1)}, u32[]{:S(2)}, u32[]{:S(2)}) %collective-permute-start.14) | collective-permute-done | bytes 262176 | tf_op jit(solution)/shard_map/ppermute | solution.py:582
  125.4 6.2 %collective-permute-done.15.refs_2_ = f32[128,512]{1,0:T(8,128)S(1)} collective-permute-done((f32[128,512]{1,0:T(8,128)S(1)}, f32[128,512]{1,0:T(8,128)S(1)}, u32[]{:S(2)}, u32[]{:S(2)}) %collective-permute-start.15) | collective-permute-done | bytes 262176 | tf_op jit(solution)/shard_map/ppermute | solution.py:582
  131.6 1.6 %unpack.1 = f32[128,4096]{1,0:T(8,128)} custom-call(f32[128,512]{1,0:T(8,128)S(1)} %get-tuple-element.97.refs_0_, f32[128,512]{1,0:T(8,128)S(1)} %collective-permute-done.14.refs_1_, f32[128,512]{1,0:T(8,128)S(1)} %collective-permute-done.15.refs_2_, f32[128,512]{1,0:T(8,128)S(1)} %collective-permute-done.16.refs_3_, ...), custom_call_target="tpu_custom_call" | custom-call | flops 3000000000 | bytes 1048576 | tf_op jit(solution)/shard_map/unpack/pallas_call | solution.py:307
  (41 shorter events, 19.7 us)
Async XLA Ops:
  0.0 6.2 %copy-start.1 = (s32[2,32]{1,0:T(2,128)S(1)}, s32[2,32]{1,0:T(2,128)}, u32[]{:S(2)}) copy-start(s32[2,32]{1,0:T(2,128)} %plan_ref.2) | copy-start | bytes 772
  0.0 6.2 %copy-start = (f32[128,4096]{1,0:T(8,128)S(1)}, f32[128,4096]{1,0:T(8,128)}, u32[]{:S(2)}) copy-start(f32[128,4096]{1,0:T(8,128)} %x_ref.3) | copy-start | bytes 6291460
  3.0 9.5 %collective-permute-start = (f32[128,512]{1,0:T(8,128)}, f32[128,512]{1,0:T(8,128)S(1)}, u32[]{:S(2)}, u32[]{:S(2)}) collective-permute-start(f32[128,512]{1,0:T(8,128)} %get-tuple-element.63), channel_id=1, source_target_pairs={{0,5},{1,4},{4,1},{5,0},{8,13},{9,12},{12,9},{13,8},{2,7},{3,6},{6... | collective-permute-start | bytes 786440 | tf_op jit(solution)/shard_map/ppermute | solution.py:582
  5.5 12.7 %collective-permute-start.1 = (f32[128,512]{1,0:T(8,128)}, f32[128,512]{1,0:T(8,128)S(1)}, u32[]{:S(2)}, u32[]{:S(2)}) collective-permute-start(f32[128,512]{1,0:T(8,128)} %get-tuple-element.64), channel_id=1, source_target_pairs={{0,4},{1,5},{4,0},{5,1},{8,12},{9,13},{12,8},{13,9},{2,6},{3,7},{6... | collective-permute-start | bytes 786440 | tf_op jit(solution)/shard_map/ppermute | solution.py:582
  6.2 12.1 %collective-permute-start.2 = (f32[128,512]{1,0:T(8,128)}, f32[128,512]{1,0:T(8,128)S(1)}, u32[]{:S(2)}, u32[]{:S(2)}) collective-permute-start(f32[128,512]{1,0:T(8,128)} %get-tuple-element.65), channel_id=1, source_target_pairs={{0,1},{1,0},{4,5},{5,4},{8,9},{9,8},{12,13},{13,12},{2,3},{3,2},{6... | collective-permute-start | bytes 786440 | tf_op jit(solution)/shard_map/ppermute | solution.py:582
  18.2 14.1 %collective-permute-start.3 = (f32[128,512]{1,0:T(8,128)S(1)}, f32[128,512]{1,0:T(8,128)S(1)}, u32[]{:S(2)}, u32[]{:S(2)}) collective-permute-start(f32[128,512]{1,0:T(8,128)S(1)} %get-tuple-element.73), channel_id=1, source_target_pairs={{0,5},{1,4},{4,1},{5,0},{8,13},{9,12},{12,9},{13,8},{2,7},{3,6},{6... | collective-permute-start | bytes 786440 | tf_op jit(solution)/shard_map/ppermute | solution.py:582
  20.2 18.3 %collective-permute-start.4 = (f32[128,512]{1,0:T(8,128)S(1)}, f32[128,512]{1,0:T(8,128)S(1)}, u32[]{:S(2)}, u32[]{:S(2)}) collective-permute-start(f32[128,512]{1,0:T(8,128)S(1)} %get-tuple-element.74), channel_id=1, source_target_pairs={{0,4},{1,5},{4,0},{5,1},{8,12},{9,13},{12,8},{13,9},{2,6},{3,7},{6... | collective-permute-start | bytes 786440 | tf_op jit(solution)/shard_map/ppermute | solution.py:582
  20.5 17.9 %collective-permute-start.5 = (f32[128,512]{1,0:T(8,128)S(1)}, f32[128,512]{1,0:T(8,128)S(1)}, u32[]{:S(2)}, u32[]{:S(2)}) collective-permute-start(f32[128,512]{1,0:T(8,128)S(1)} %get-tuple-element.75), channel_id=1, source_target_pairs={{0,1},{1,0},{4,5},{5,4},{8,9},{9,8},{12,13},{13,12},{2,3},{3,2},{6... | collective-permute-start | bytes 786440 | tf_op jit(solution)/shard_map/ppermute | solution.py:582
  21.6 20.1 %collective-permute-start.6 = (f32[264,256]{1,0:T(8,128)S(1)}, f32[264,256]{1,0:T(8,128)S(1)}, u32[]{:S(2)}, u32[]{:S(2)}) collective-permute-start(f32[264,256]{1,0:T(8,128)S(1)} %get-tuple-element.77.refs_0_), channel_id=1, source_target_pairs={{0,8},{8,0},{1,9},{9,1},{4,12},{12,4},{5,13},{13,5},{7,15},{15,7},... | collective-permute-start | bytes 811016 | tf_op jit(solution)/shard_map/ppermute | solution.py:599
  39.4 17.4 %collective-permute-start.7 = (f32[264,256]{1,0:T(8,128)S(1)}, f32[264,256]{1,0:T(8,128)S(1)}, u32[]{:S(2)}, u32[]{:S(2)}) collective-permute-start(f32[264,256]{1,0:T(8,128)S(1)} %get-tuple-element.79.refs_0_), channel_id=1, source_target_pairs={{0,8},{8,0},{1,9},{9,1},{4,12},{12,4},{5,13},{13,5},{7,15},{15,7},... | collective-permute-start | bytes 811016 | tf_op jit(solution)/shard_map/ppermute | solution.py:599
  54.2 8.2 %collective-permute-start.8 = (f32[512,256]{1,0:T(8,128)S(1)}, f32[512,256]{1,0:T(8,128)S(1)}, u32[]{:S(2)}, u32[]{:S(2)}) collective-permute-start(f32[512,256]{1,0:T(8,128)S(1)} %turn.5.refs_0_), channel_id=1, source_target_pairs={{1,0},{9,8},{4,1},{12,9},{5,4},{13,12},{7,5},{15,13},{6,7},{14,15}... | collective-permute-start | bytes 1572872 | tf_op jit(solution)/shard_map/ppermute | solution.py:608
  63.6 17.1 %collective-permute-start.11 = (f32[264,256]{1,0:T(8,128)S(1)}, f32[264,256]{1,0:T(8,128)S(1)}, u32[]{:S(2)}, u32[]{:S(2)}) collective-permute-start(f32[264,256]{1,0:T(8,128)S(1)} %get-tuple-element.87.old_terms_ref), channel_id=1, source_target_pairs={{0,8},{8,0},{1,9},{9,1},{4,12},{12,4},{5,13},{13,5},{7,15},{15,7},... | collective-permute-start | bytes 811016 | tf_op jit(solution)/shard_map/ppermute | solution.py:599
  71.4 9.3 %collective-permute-start.12 = (f32[264,256]{1,0:T(8,128)S(1)}, f32[264,256]{1,0:T(8,128)S(1)}, u32[]{:S(2)}, u32[]{:S(2)}) collective-permute-start(f32[264,256]{1,0:T(8,128)S(1)} %get-tuple-element.102.refs_0_), channel_id=1, source_target_pairs={{2,10},{10,2},{18,26},{26,18}} | collective-permute-start | bytes 811016 | tf_op jit(solution)/shard_map/ppermute | solution.py:599
  73.1 7.6 %collective-permute-start.9 = (f32[256,256]{1,0:T(8,128)S(1)}, f32[256,256]{1,0:T(8,128)S(1)}, u32[]{:S(2)}, u32[]{:S(2)}) collective-permute-start(f32[256,256]{1,0:T(8,128)S(1)} %get-tuple-element.90), channel_id=1, source_target_pairs={{0,1},{8,9},{1,4},{9,12},{4,5},{12,13},{5,7},{13,15},{7,6},{15,14}... | collective-permute-start | bytes 786440 | tf_op jit(solution)/shard_map/ppermute | solution.py:608
  77.3 3.4 %collective-permute-start.10 = (f32[256,256]{1,0:T(8,128)S(1)}, f32[256,256]{1,0:T(8,128)S(1)}, u32[]{:S(2)}, u32[]{:S(2)}) collective-permute-start(f32[256,256]{1,0:T(8,128)S(1)} %get-tuple-element.91), channel_id=1, source_target_pairs={{0,1},{8,9},{1,4},{9,12},{4,5},{12,13},{5,7},{13,15},{7,6},{15,14}... | collective-permute-start | bytes 786440 | tf_op jit(solution)/shard_map/ppermute | solution.py:608
  81.9 22.9 %collective-permute-start.13 = (f32[264,256]{1,0:T(8,128)S(1)}, f32[264,256]{1,0:T(8,128)S(1)}, u32[]{:S(2)}, u32[]{:S(2)}) collective-permute-start(f32[264,256]{1,0:T(8,128)S(1)} %get-tuple-element.96.refs_0_), channel_id=1, source_target_pairs={{0,8},{8,0},{1,9},{9,1},{4,12},{12,4},{5,13},{13,5},{7,15},{15,7},... | collective-permute-start | bytes 811016 | tf_op jit(solution)/shard_map/ppermute | solution.py:599
  97.4 23.5 %collective-permute-start.17 = (f32[128,512]{1,0:T(8,128)S(1)}, f32[128,512]{1,0:T(8,128)S(1)}, u32[]{:S(2)}, u32[]{:S(2)}) collective-permute-start(f32[128,512]{1,0:T(8,128)S(1)} %get-tuple-element.104), channel_id=1, source_target_pairs={{0,5},{1,4},{4,1},{5,0},{8,13},{9,12},{12,9},{13,8},{2,7},{3,6},{6... | collective-permute-start | bytes 786440 | tf_op jit(solution)/shard_map/ppermute | solution.py:582
  101.9 19.0 %collective-permute-start.18 = (f32[128,512]{1,0:T(8,128)S(1)}, f32[128,512]{1,0:T(8,128)S(1)}, u32[]{:S(2)}, u32[]{:S(2)}) collective-permute-start(f32[128,512]{1,0:T(8,128)S(1)} %get-tuple-element.105), channel_id=1, source_target_pairs={{0,4},{1,5},{4,0},{5,1},{8,12},{9,13},{12,8},{13,9},{2,6},{3,7},{6... | collective-permute-start | bytes 786440 | tf_op jit(solution)/shard_map/ppermute | solution.py:582
  104.7 16.3 %collective-permute-start.19 = (f32[128,512]{1,0:T(8,128)S(1)}, f32[128,512]{1,0:T(8,128)S(1)}, u32[]{:S(2)}, u32[]{:S(2)}) collective-permute-start(f32[128,512]{1,0:T(8,128)S(1)} %get-tuple-element.106), channel_id=1, source_target_pairs={{0,1},{1,0},{4,5},{5,4},{8,9},{9,8},{12,13},{13,12},{2,3},{3,2},{6... | collective-permute-start | bytes 786440 | tf_op jit(solution)/shard_map/ppermute | solution.py:582
  117.3 8.1 %collective-permute-start.14 = (f32[128,512]{1,0:T(8,128)S(1)}, f32[128,512]{1,0:T(8,128)S(1)}, u32[]{:S(2)}, u32[]{:S(2)}) collective-permute-start(f32[128,512]{1,0:T(8,128)S(1)} %get-tuple-element.98), channel_id=1, source_target_pairs={{0,5},{1,4},{4,1},{5,0},{8,13},{9,12},{12,9},{13,8},{2,7},{3,6},{6... | collective-permute-start | bytes 786440 | tf_op jit(solution)/shard_map/ppermute | solution.py:582
  120.1 11.5 %collective-permute-start.15 = (f32[128,512]{1,0:T(8,128)S(1)}, f32[128,512]{1,0:T(8,128)S(1)}, u32[]{:S(2)}, u32[]{:S(2)}) collective-permute-start(f32[128,512]{1,0:T(8,128)S(1)} %get-tuple-element.99), channel_id=1, source_target_pairs={{0,4},{1,5},{4,0},{5,1},{8,12},{9,13},{12,8},{13,9},{2,6},{3,7},{6... | collective-permute-start | bytes 786440 | tf_op jit(solution)/shard_map/ppermute | solution.py:582
  120.9 10.7 %collective-permute-start.16 = (f32[128,512]{1,0:T(8,128)S(1)}, f32[128,512]{1,0:T(8,128)S(1)}, u32[]{:S(2)}, u32[]{:S(2)}) collective-permute-start(f32[128,512]{1,0:T(8,128)S(1)} %get-tuple-element.100), channel_id=1, source_target_pairs={{0,1},{1,0},{4,5},{5,4},{8,9},{9,8},{12,13},{13,12},{2,3},{3,2},{6... | collective-permute-start | bytes 786440 | tf_op jit(solution)/shard_map/ppermute | solution.py:582
